TPU v7x, 512 devices: a whole 4x8x8 slice. The times are simulated.
512 devices in a mesh: section: 8 (over y_hi, core), dp: 64 (over x, z, y_lo).
Axes of the slice: x: 4, y: 8 (y_hi: 4, y_lo: 2; y = y_hi * 2 + y_lo), z: 8, core: 2. Of those that a mesh axis runs over, the one named last changes fastest.
Arguments:
- inputs: bfloat16 [2, 4096, 4096], P(None, 'dp'), may hold values from -6 to 6
- cotangent: bfloat16 [2, 4096, 4096], P(None, 'dp'), may hold values from -6 to 6
- doc_lengths: int32 [2, 64, 2], P(None, 'dp'), may hold values from 1 to 48, 64 in all within a row
- norm_gain: bfloat16 [8, 4096], P('section'), may hold values from 0.25 to 1.75
- w_qkv: bfloat16 [8, 4096, 192], P('section', 'dp'), may hold values from -0.09375 to 0.09375
- w_out: bfloat16 [8, 64, 4096], P('section', None, 'dp'), may hold values from -0.75 to 0.75
Outputs:
- grad_qkv: float32 [8, 4096, 192], P('section', 'dp')
- grad_out: float32 [8, 64, 4096], P('section', None, 'dp')
Inputs may be any that keep to these rules, and one draw needn't show every extreme that they name: `doc_lengths`: each row's 2 lengths add up to 64.
All inputs are finite; a program needn't handle non-finite values.
Results may differ from a plain program's by a relative error of at most 0.025.
Values may be sent and summed in bfloat16 or wider, within the bound.
A program may use at most 64 MiB of HBM per device.

v0:
```python
import jax
import jax.numpy as jnp
from jax import lax
from jax.sharding import PartitionSpec as P


def passed_along(block, axis, distance):
    devices = range(lax.axis_size(axis))
    route = [(i - distance, i) for i in devices if i - distance in devices]
    return lax.ppermute(block, axis, route)


def segments_of(lengths, count):
    ends = jnp.cumsum(lengths)
    position = jnp.arange(count, dtype=jnp.int32)
    return jnp.sum((position[:, None] >= ends[None, :]).astype(jnp.int32), axis=1)


def layer(x, gain, w_qkv, w_out, seg):
    head = w_out.shape[0]
    x_wide = x.astype(jnp.float32)
    scale = lax.rsqrt(jnp.mean(x_wide * x_wide, axis=-1, keepdims=True) + 1e-05)
    normed = (x_wide * scale * gain.astype(jnp.float32)).astype(jnp.bfloat16)
    qkv = jnp.dot(normed, w_qkv, preferred_element_type=jnp.float32).astype(jnp.bfloat16)
    query = qkv[:, :head]
    keys = qkv[:, head : 2 * head]
    values = qkv[:, 2 * head :]
    scores = jnp.dot(query, keys.T, preferred_element_type=jnp.float32) * head ** (-0.5)
    rows = jnp.arange(x.shape[0], dtype=jnp.int32)
    allowed = (seg[:, None] == seg[None, :]) & (rows[:, None] >= rows[None, :])
    scores = jnp.where(allowed, scores, -1e30)
    probs = jax.nn.softmax(scores, axis=-1).astype(jnp.bfloat16)
    attended = jnp.dot(probs, values, preferred_element_type=jnp.float32).astype(jnp.bfloat16)
    return (x_wide + jnp.dot(attended, w_out, preferred_element_type=jnp.float32)).astype(
        jnp.bfloat16
    )


def body(inputs, cotangent, doc_lengths, norm_gain, w_qkv, w_out):
    sections = lax.axis_size("section")
    section = lax.axis_index("section")
    micro = inputs.shape[0]
    count = inputs.shape[1]
    segs = jax.vmap(lambda lens: segments_of(lens, count))(doc_lengths[:, 0, :])
    gain = norm_gain[0]
    full_qkv, full_out = (
        lax.all_gather(w_qkv[0], "dp", axis=0, tiled=True),
        lax.all_gather(w_out[0], "dp", axis=1, tiled=True),
    )
    total_steps = micro + sections - 1
    empty = jnp.zeros(inputs.shape[1:], inputs.dtype)

    def forward_at(step, incoming, saved):
        index = step - section
        live = (index >= 0) & (index < micro)
        slot = jnp.clip(index, 0, micro - 1)
        first = lax.dynamic_index_in_dim(inputs, slot, 0, keepdims=False)
        x = jnp.where(section == 0, first, incoming)
        seg = lax.dynamic_index_in_dim(segs, slot, 0, keepdims=False)
        out = layer(x, gain, full_qkv, full_out, seg)
        old = lax.dynamic_index_in_dim(saved, slot, 0, keepdims=False)
        saved = lax.dynamic_update_index_in_dim(saved, jnp.where(live, x, old), slot, 0)
        return (out, saved)

    def forward_step(carry, step):
        incoming, saved = carry
        out, saved = forward_at(step, incoming, saved)
        incoming = passed_along(out, "section", 1)
        return ((incoming, saved), None)

    start_saved = jnp.zeros(inputs.shape, inputs.dtype)
    (incoming, saved), _ = lax.scan(
        forward_step, (empty, start_saved), jnp.arange(total_steps - 1, dtype=jnp.int32)
    )
    _, saved = forward_at(jnp.int32(total_steps - 1), incoming, saved)
    back_qkv, back_out = (
        lax.all_gather(w_qkv[0], "dp", axis=0, tiled=True),
        lax.all_gather(w_out[0], "dp", axis=1, tiled=True),
    )

    def backward_at(step, incoming, sum_qkv, sum_out):
        index = step - (sections - 1 - section)
        live = (index >= 0) & (index < micro)
        slot = jnp.clip(index, 0, micro - 1)
        last = lax.dynamic_index_in_dim(cotangent, slot, 0, keepdims=False)
        grad_y = jnp.where(section == sections - 1, last, incoming)
        x = lax.dynamic_index_in_dim(saved, slot, 0, keepdims=False)
        seg = lax.dynamic_index_in_dim(segs, slot, 0, keepdims=False)
        _, pull = jax.vjp(lambda a, b, c: layer(a, gain, b, c, seg), x, back_qkv, back_out)
        grad_x, grad_q, grad_o = pull(grad_y)
        sum_qkv = sum_qkv + jnp.where(live, grad_q.astype(jnp.float32), 0.0)
        sum_out = sum_out + jnp.where(live, grad_o.astype(jnp.float32), 0.0)
        return (grad_x, sum_qkv, sum_out)

    def backward_step(carry, step):
        incoming, sum_qkv, sum_out = carry
        grad_x, sum_qkv, sum_out = backward_at(step, incoming, sum_qkv, sum_out)
        incoming = passed_along(grad_x, "section", -1)
        return ((incoming, sum_qkv, sum_out), None)

    zero_qkv = jnp.zeros(back_qkv.shape, jnp.float32)
    zero_out = jnp.zeros(back_out.shape, jnp.float32)
    (incoming, sum_qkv, sum_out), _ = lax.scan(
        backward_step, (empty, zero_qkv, zero_out), jnp.arange(total_steps - 1, dtype=jnp.int32)
    )
    _, sum_qkv, sum_out = backward_at(jnp.int32(total_steps - 1), incoming, sum_qkv, sum_out)
    share_qkv, share_out = (
        lax.psum_scatter(sum_qkv, "dp", scatter_dimension=0, tiled=True),
        lax.psum_scatter(sum_out, "dp", scatter_dimension=1, tiled=True),
    )
    return (share_qkv[None], share_out[None])


def solution(mesh):
    return jax.shard_map(
        body,
        mesh=mesh,
        in_specs=(
            P(None, "dp", None),
            P(None, "dp", None),
            P(None, "dp", None),
            P("section", None),
            P("section", "dp", None),
            P("section", None, "dp"),
        ),
        out_specs=(P("section", "dp", None), P("section", None, "dp")),
        check_vma=False,
    )
```

profile of v0, /device:TPU:16, one launch (start us, length us, event | category | flops | bytes accessed | tf_op | source)
XLA Modules:
  0.0 1309.9 jit_solution(11713632534645186579)
XLA Ops:
  9.7 185.1 %all-gather.1 = bf16[1,64,4096]{1,0,2:T(2,128)(2,1)S(1)} all-gather(bf16[1,64,64]{1,0,2:T(2,128)(2,1)S(1)} %copy.16), channel_id=3, replica_groups=mesh['section'=8,'dp'=64] {'dp'}, dimensions={2}, use_global_device_ids=true | all-gather | bytes 532480 | tf_op jit(solution)/shard_map/all_gather | solution.py:48
  194.7 3.6 copy.17
  198.5 120.8 %all-gather.4.cloned.1.call-done = bf16[1,4096,192]{2,1,0:T(8,128)(2,1)} async-done(((bf16[1,64,192]{2,1,0:T(8,128)(2,1)}), bf16[1,4096,192]{2,1,0:T(8,128)(2,1)}) %all-gather.4.cloned.1.call-update) | async-done | bytes 1572880 | tf_op jit(solution)/shard_map/all_gather | solution.py:47
  320.3 157.4 %while.30 = (s32[]{:T(128)}, bf16[64,4096]{1,0:T(8,128)(2,1)}, bf16[2,64,4096]{2,1,0:T(8,128)(2,1)S(1)}, pred[]{:T(512)}, s32[8]{0:T(128)S(1)}, /*index=5*/s32[]...) while((s32[]{:T(128)}, bf16[64,4096]{1,0:T(8,128)(2,1)}, ...), condition=%wide.region_6.7_spmd, body=%wide.region_2.6_spmd.sunk | while | flops 138477504 | bytes 20632148 | solution.py:72
  326.7 1.9 collective-permute-start
  328.6 9.6 collective-permute-done
  345.4 1.9 collective-permute-start
  347.3 9.6 collective-permute-done
  364.1 12.1 collective-permute-start
  384.8 11.2 collective-permute-start
  404.7 11.1 collective-permute-start
  424.6 11.1 collective-permute-start
  444.4 11.1 collective-permute-start
  464.2 11.2 collective-permute-start
  481.1 157.0 %while.31 = (s32[]{:T(128)}, bf16[64,4096]{1,0:T(8,128)(2,1)}, f32[4096,192]{0,1:T(8,128)}, f32[64,4096]{1,0:T(8,128)}, pred[]{:T(512)}, /*index=5*/s32[8]{0:T(1...) while((s32[]{:T(128)}, bf16[64,4096]{1,0:T(8,128)(2,1)}, ...), condition=%wide.region_13.14_spmd.clone, body=%wide.region_7.13_spmd.clone.sunk | while | flops 384602496 | bytes 32000636 | solution.py:103
  487.8 1.9 collective-permute-start.1
  489.7 2.6 fusion.168
  492.2 2.4 fusion.167
  494.6 6.0 collective-permute-done.1
  507.3 1.9 collective-permute-start.1
  509.2 2.9 fusion.168
  512.1 4.3 fusion.167
  516.4 4.6 collective-permute-done.1
  527.6 1.9 collective-permute-start.1
  529.5 2.9 fusion.168
  532.4 4.3 fusion.167
  536.6 3.8 collective-permute-done.1
  549.0 2.9 fusion.168
  551.9 4.3 fusion.167
  556.2 3.8 collective-permute-done.1
  568.5 2.9 fusion.168
  571.4 4.3 fusion.167
  575.7 3.8 collective-permute-done.1
  588.1 2.9 fusion.168
  591.0 4.3 fusion.167
  595.2 3.8 collective-permute-done.1
  607.6 2.9 fusion.168
  610.5 4.3 fusion.167
  614.8 3.8 collective-permute-done.1
  627.1 2.9 fusion.168
  630.0 4.3 fusion.167
  634.3 3.8 collective-permute-done.1
  638.1 2.1 fusion.56
  640.2 2.0 copy.19
  642.3 5.2 copy.18
  649.6 5.0 fusion.53
  654.6 323.6 %reduce-scatter.7.cloned.1.call-done = f32[64,64]{1,0:T(8,128)} async-done(((f32[4096,64]{1,0:T(8,128)}), f32[64,64]{1,0:T(8,128)}) %reduce-scatter.7.cloned.1.call-update) | async-done | bytes 16400
  979.7 323.7 %reduce-scatter.5.cloned.1.call-done = f32[64,192]{1,0:T(8,128)} async-done(((f32[4096,192]{1,0:T(8,128)}), f32[64,192]{1,0:T(8,128)}) %reduce-scatter.5.cloned.1.call-update) | async-done | bytes 49168 | tf_op jit(solution)/shard_map/reduce_scatter | solution.py:108
  (398 shorter events, 128.2 us)
Async XLA Ops:
  7.2 191.2 %copy-start.9 = (bf16[1,4096]{1,0:T(2,128)(2,1)S(1)}, bf16[1,4096]{1,0:T(2,128)(2,1)}, u32[]{:S(2)}) copy-start(bf16[1,4096]{1,0:T(2,128)(2,1)} %param.13) | copy-start | bytes 24580
  7.2 312.2 %all-gather.4.cloned.1.call-start = ((), (), s32[]{:S(2)}) async-start(), calls=%async_computation.3 | async-start | bytes 2129920 | tf_op jit(solution)/shard_map/all_gather | solution.py:47
  7.9 970.3 %reduce-scatter.7.cloned.1.call-start = ((), (), s32[]{:S(2)}) async-start(), calls=%async_computation.4 | async-start | bytes 2129920
  320.3 3.9 copy-start
  326.7 11.5 collective-permute-start
  339.0 3.9 copy-start
  345.4 11.5 collective-permute-start
  357.6 3.9 copy-start
  364.1 13.6 %collective-permute-start = (bf16[64,4096]{1,0:T(8,128)(2,1)S(1)}, bf16[64,4096]{1,0:T(8,128)(2,1)S(1)}, u32[]{:S(2)}, u32[]{:S(2)}) collective-permute-start(bf16[64,4096]{1,0:T(8,128)(2,1)S(1)} %fusion.145), channel_id=1, source_target_pairs={{0,64},{64,128},{128,192},{192,256},{256,320},{320,384},{384,448},... | collective-permute-start | bytes 1572872 | tf_op jit(solution)/shard_map/while/body/eval_jaxpr/ppermute | solution.py:10
  378.4 3.9 copy-start
  384.8 12.7 collective-permute-start
  398.3 3.9 copy-start
  404.7 12.7 collective-permute-start
  418.2 3.9 copy-start
  424.6 12.6 collective-permute-start
  438.0 3.9 copy-start
  444.4 12.6 collective-permute-start
  457.8 3.9 copy-start
  464.2 12.7 collective-permute-start
  477.6 1.9 copy-start.1
  482.4 1.2 copy-start.7
  482.4 2.3 copy-start.4
  484.7 3.0 copy-start.2
  487.8 12.9 collective-permute-start.1
  501.9 2.3 copy-start.4
  504.2 3.0 copy-start.2
  507.3 13.7 %collective-permute-start.1 = (bf16[64,4096]{1,0:T(8,128)(2,1)}, bf16[64,4096]{1,0:T(8,128)(2,1)}, u32[]{:S(2)}, u32[]{:S(2)}) collective-permute-start(bf16[64,4096]{1,0:T(8,128)(2,1)} %fusion.166), channel_id=1, source_target_pairs={{64,0},{128,64},{192,128},{256,192},{320,256},{384,320},{448,384},... | collective-permute-start | bytes 1572872 | tf_op jit(solution)/shard_map/while/body/eval_jaxpr/ppermute | solution.py:10
  522.2 2.3 copy-start.4
  524.5 3.0 copy-start.2
  527.6 12.9 collective-permute-start.1
  541.7 2.3 copy-start.4
  544.0 3.0 copy-start.2
  547.1 12.9 collective-permute-start.1
  561.3 2.3 copy-start.4
  563.6 3.0 copy-start.2
  566.6 12.9 collective-permute-start.1
  580.8 2.3 copy-start.4
  583.1 3.0 copy-start.2
  586.1 12.9 collective-permute-start.1
  600.3 2.3 copy-start.4
  602.6 3.0 copy-start.2
  605.7 12.9 collective-permute-start.1
  619.8 2.3 copy-start.4
  622.2 3.0 copy-start.2
  625.2 12.9 collective-permute-start.1
  642.2 661.2 %reduce-scatter.5.cloned.1.call-start = ((), (), s32[]{:S(2)}) async-start(), calls=%async_computation.2 | async-start | bytes 4259840 | tf_op jit(solution)/shard_map/reduce_scatter | solution.py:108
  642.2 5.3 copy-start.5
  642.3 5.3 copy-start.8
  (23 other events, 21.2 us)
Sparse Core Ops, SparseCore 0:
  10.1 309.1 all-gather.3
  642.3 335.8 reduce-scatter.6
  981.8 321.5 reduce-scatter.4
where the time goes:
time: 1310 us
  waiting for transfers between devices  831 us (63%)
  blocking collectives  185 us (14%)
  matrix products  104 us (8%)
  starting transfers between devices  87 us (7%)
  local copies, waits for them, and re-layouts  39.2 us (3%)
  other arithmetic  38.6 us (3%)
  between operations  13.9 us (1%)
    unnamed x4, waiting for transfers between devices  324 us
    reduce_scatter x1, waiting for transfers between devices, body(): lax.psum_scatter(sum_qkv, 'dp', scatter_dimension=0, tiled=True)  324 us
    all_gather x1, blocking collectives, body(): lax.all_gather(w_out[0], 'dp', axis=1, tiled=True)  185 us
    all_gather x1, waiting for transfers between devices, body(): lax.all_gather(w_qkv[0], 'dp', axis=0, tiled=True)  121 us
    ppermute x16, starting transfers between devices, passed_along(): return lax.ppermute(block, axis, route)  86.9 us
    ppermute x16, waiting for transfers between devices, passed_along(): return lax.ppermute(block, axis, route)  61.8 us
    dot_general x34, matrix products, layer(): jnp.dot(normed, w_qkv, preferred_element_type=jnp.float32)  52.9 us
    dot_general x26, matrix products, layer(): jnp.dot(attended, w_out, preferred_element_type=jnp.float32)  41.8 us
  transfers between devices with their start and end apart: 19, of which 19 were waited for; matrix products, arithmetic and copies ran while one was open for 6% of the time, Pallas kernels for 0%

commit v1 on v0

v1 whole, which is shorter than its diff:
```python
import functools

import jax
import jax.numpy as jnp
from jax import lax
from jax.experimental import pallas as pl
from jax.experimental.pallas import tpu as pltpu
from jax.sharding import PartitionSpec as P

MESH = pl.DeviceIdType.MESH
F32, BF16 = jnp.float32, jnp.bfloat16
SUB = 16


def nn(a, b):
    return jnp.dot(a, b, preferred_element_type=F32)


def nt(a, b):
    return lax.dot_general(a, b, (((1,), (1,)), ((), ())), preferred_element_type=F32)


def tn(a, b):
    return lax.dot_general(a, b, (((0,), (0,)), ((), ())), preferred_element_type=F32)


def kernel(
    nc, nx, nz, rows,
    inp, cot, lens, wg, out,
    W, xin, cin, X, DY, QK, KK, VV, PR, ATT, SC, SD,
    es, er, bs, br, G, SR, H, XR, H2, ZR, H3, YR, FS, OB,
    in_sem, s1_s, s1_r, y_s, y_r, z_s, z_r, x_s, x_r, c_s, c_r,
    e_s, e_r, b_s, b_r, rc_s, rc_r, rx_s, rx_r, rz_s, rz_r, ry_s, ry_r, f_s, f_r,
):
    layers = 2 * nc
    dps = nx * nz * 2
    local = SUB * dps
    width = local * nc
    zrows, xrows = 2 * SUB, 2 * SUB * nz
    s, d = lax.axis_index("section"), lax.axis_index("dp")
    c, k = lax.div(s, 2), lax.rem(s, 2)
    x, z, y = lax.div(d, 2 * nz), lax.rem(lax.div(d, 2), nz), lax.rem(d, 2)

    def at(start, size):
        return pl.ds(pl.multiple_of(start, SUB), size)

    def section_peer(o):
        return lax.rem(s + o, layers)

    def chip_peer(o):
        return (2 * lax.rem(c + o, nc) + k, d)

    def x_peer(o):
        return lax.rem(x + o, nx)

    def z_peer(o):
        return lax.rem(z + o, nz)

    def dp_of(px, pz, py):
        return (px * nz + pz) * 2 + py

    sibling = (2 * c + 1 - k, d)
    y_partner = (s, dp_of(x, z, 1 - y))

    def send(src, dst, send_sem, recv_sem, device):
        pltpu.make_async_remote_copy(
            src_ref=src, dst_ref=dst, send_sem=send_sem, recv_sem=recv_sem,
            device_id=device, device_id_type=MESH,
        ).start()

    def wait(ref, sem):
        pltpu.make_async_copy(ref, ref, sem).wait()

    load_x = pltpu.make_async_copy(inp.at[k], xin, in_sem.at[0])
    load_c = pltpu.make_async_copy(cot.at[k], cin, in_sem.at[1])
    own = pltpu.make_async_copy(
        wg.at[k, at(SUB * c, SUB)], W.at[k, s, at(SUB * d, SUB)], in_sem.at[2]
    )
    load_x.start()
    load_c.start()
    own.start()

    barrier = pltpu.get_barrier_semaphore()
    peers = [(section_peer(o), d) for o in range(1, layers)]
    peers += [(s, dp_of(x_peer(o), z, y)) for o in range(1, nx)]
    peers += [(s, dp_of(x, z_peer(o), y)) for o in range(1, nz)]
    peers += [y_partner]
    for peer in peers:
        pl.semaphore_signal(barrier, inc=1, device_id=peer, device_id_type=MESH)
    pl.semaphore_wait(barrier, len(peers))

    for o in range(1, layers):
        t = section_peer(o)
        tc, tk = lax.div(t, 2), lax.rem(t, 2)
        send(
            wg.at[tk, at(SUB * tc, SUB)], W.at[tk, s, at(SUB * d, SUB)],
            s1_s, s1_r, (t, d),
        )

    load_x.wait()
    load_c.wait()
    grain = min(8, dps)
    big, small = grain * SUB * nc, grain * SUB
    at_row = lax.broadcasted_iota(jnp.int32, (big, small), 0)
    at_lane = lax.broadcasted_iota(jnp.int32, (big, small), 1)
    wanted = lax.div(at_lane, SUB) * (SUB * nc) + lax.rem(at_lane, SUB) + SUB * c
    pick = jnp.where(at_row == wanted, 1.0, 0.0).astype(BF16)
    for m in range(dps // grain):
        X[0, :, m * small : (m + 1) * small] = nn(
            xin[:, m * big : (m + 1) * big], pick
        ).astype(BF16)
        DY[layers - 1, :, m * small : (m + 1) * small] = nn(
            cin[:, m * big : (m + 1) * big], pick
        ).astype(BF16)

    own.wait()
    wait(W.at[0, 0, pl.ds(0, SUB * (layers - 1))], s1_r)
    mine = W.at[k, :, at(SUB * d, SUB)]
    send(mine, mine, y_s, y_r, y_partner)
    wait(mine, y_r)

    def z_gather(l):
        block = W.at[k, l, at(zrows * (x * nz + z), zrows)]
        for o in range(1, nz):
            send(block, block, z_s, z_r.at[l], (s, dp_of(x, z_peer(o), y)))

    def x_gather(l):
        if nz > 1:
            wait(W.at[0, 0, pl.ds(0, zrows * (nz - 1))], z_r.at[l])
        block = W.at[k, l, at(xrows * x, xrows)]
        for o in range(1, nx):
            send(block, block, x_s, x_r.at[l], (s, dp_of(x_peer(o), z, y)))

    def core_gather(l):
        if nx > 1:
            wait(W.at[0, 0, pl.ds(0, xrows * (nx - 1))], x_r.at[l])
        send(W.at[k, l], W.at[k, l], c_s, c_r.at[l], sibling)

    row = lax.broadcasted_iota(jnp.int32, (rows, rows), 0)
    col = lax.broadcasted_iota(jnp.int32, (rows, rows), 1)
    first = lens[k, 0]
    allowed = ((row < first) == (col < first)) & (row >= col)
    lane = lax.broadcasted_iota(jnp.int32, (rows, 128), 1)
    low = lane < 64

    def both(l):
        return jnp.concatenate([W[0, l], W[1, l]], axis=1)

    def forward(l, between):
        slot = lax.rem(l, 2)
        wait(W.at[0, 0], c_r.at[l])
        xb = X[l]
        part = nn(xb, both(l))
        wide = xb.astype(F32)
        square = jnp.sum(wide * wide, axis=1, keepdims=True)
        upper = square.astype(BF16).astype(F32)
        es[slot, :, :128] = part[:, :128].astype(BF16)
        tail = jnp.where(lane < 96, upper, square - upper)
        es[slot, :, 128:] = jnp.where(low, part[:, 128:], tail).astype(BF16)
        for o in range(1, nc):
            send(es.at[slot], er.at[slot, o - 1], e_s.at[slot], e_r.at[slot], chip_peer(o))
        between(l)
        t0, t1 = part[:, :128], part[:, 128:]
        if nc > 1:
            wait(er.at[slot], e_r.at[slot])
            for o in range(nc - 1):
                t0 = t0 + er[slot, o, :, :128].astype(F32)
                more = er[slot, o, :, 128:].astype(F32)
                t1 = t1 + more
                square = square + more[:, 64:65] + more[:, 96:97]
            wait(er.at[slot], e_s.at[slot])
        scale = lax.rsqrt(square * (1.0 / width) + 1e-05)
        q = t0 * scale
        kk = pltpu.roll(q, 64, 1).astype(BF16)
        vv = pltpu.roll(jnp.where(low, t1 * scale, 0.0), 64, 1).astype(BF16)
        scores = nt(jnp.where(low, q, 0.0).astype(BF16), kk) * 0.125
        scores = jnp.where(allowed, scores, -1e30)
        top = jnp.max(scores, axis=1, keepdims=True)
        e = jnp.exp(scores - top)
        p = e / jnp.sum(e, axis=1, keepdims=True)
        att = nn(p.astype(BF16), vv).astype(BF16)
        QK[l] = q.astype(BF16)
        KK[l] = kk
        VV[l] = vv
        PR[l] = p
        ATT[l] = att
        SC[l] = jnp.broadcast_to(scale, (rows, 128))

        @pl.when(l < layers - 1)
        def _():
            X[l + 1] = (X[l].astype(F32) + nt(att, W[1, l])).astype(BF16)

    def ahead(l):
        @pl.when(l + 3 < layers)
        def _():
            z_gather(l + 3)

        @pl.when(l + 2 < layers)
        def _():
            x_gather(l + 2)

        @pl.when(l + 1 < layers)
        def _():
            core_gather(l + 1)

    z_gather(0)
    if layers > 1:
        z_gather(1)
    x_gather(0)
    if layers > 2:
        z_gather(2)
    if layers > 1:
        x_gather(1)
    core_gather(0)

    def forward_step(l, carry):
        forward(l, ahead)
        return carry

    lax.fori_loop(0, layers, forward_step, 0)

    def grads(l):
        left = jnp.concatenate([X[l], DY[l]], axis=0)
        att = ATT[l]
        right = jnp.concatenate(
            [
                jnp.concatenate([SD[l, 0], SD[l, 1]], axis=1),
                jnp.concatenate([jnp.zeros_like(att), att], axis=1),
            ],
            axis=0,
        )
        g = tn(left, right)
        G[l, 0] = g[:, :128].astype(BF16)
        G[l, 1] = g[:, 128:].astype(BF16)
        send(G.at[l, 1 - k], SR.at[l], rc_s, rc_r.at[l], sibling)

    def x_scatter(l):
        wait(SR.at[l], rc_r.at[l])
        H[l] = (G[l, k].astype(F32) + SR[l].astype(F32)).astype(BF16)
        for o in range(1, nx):
            px = x_peer(o)
            send(
                H.at[l, at(xrows * px, xrows)], XR.at[l, o - 1],
                rx_s, rx_r.at[l], (s, dp_of(px, z, y)),
            )

    def z_scatter(l):
        total = H[l, at(xrows * x, xrows)].astype(F32)
        if nx > 1:
            wait(XR.at[l], rx_r.at[l])
            for o in range(nx - 1):
                total = total + XR[l, o].astype(F32)
        H2[l] = total.astype(BF16)
        for o in range(1, nz):
            pz = z_peer(o)
            send(
                H2.at[l, at(zrows * pz, zrows)], ZR.at[l, o - 1],
                rz_s, rz_r.at[l], (s, dp_of(x, pz, y)),
            )

    def y_scatter(l):
        total = H2[l, at(zrows * z, zrows)].astype(F32)
        if nz > 1:
            wait(ZR.at[l], rz_r.at[l])
            for o in range(nz - 1):
                total = total + ZR[l, o].astype(F32)
        H3[l] = total.astype(BF16)
        send(H3.at[l, at(SUB * (1 - y), SUB)], YR.at[l], ry_s, ry_r.at[l], y_partner)

    def finish(l):
        wait(YR.at[l], ry_r.at[l])
        FS[l] = H3[l, at(SUB * y, SUB)].astype(F32) + YR[l].astype(F32)

    def staged(l, behind, stage):
        @pl.when((l + behind >= 0) & (l + behind < layers))
        def _():
            stage(l + behind)

    def backward_step(step, carry):
        l = layers - 1 - step
        slot = lax.rem(step, 2)

        @pl.when(l >= 0)
        def _():
            part = nn(DY[l], W[1, l])
            bs[slot] = part.astype(BF16)
            for o in range(1, nc):
                send(bs.at[slot], br.at[slot, o - 1], b_s.at[slot], b_r.at[slot], chip_peer(o))

        staged(l, 1, grads)
        staged(l, 2, x_scatter)
        staged(l, 3, z_scatter)
        staged(l, 4, y_scatter)
        staged(l, 5, finish)

        @pl.when(l >= 0)
        def _():
            total = bs[slot].astype(F32)
            if nc > 1:
                wait(br.at[slot], b_r.at[slot])
                for o in range(nc - 1):
                    total = total + br[slot, o].astype(F32)
                wait(br.at[slot], b_s.at[slot])
            da = jnp.where(low, 0.0, total).astype(BF16)
            vv, kk, p, scale = VV[l], KK[l], PR[l], SC[l]
            dp = nt(da, vv)
            ds = p * (dp - jnp.sum(p * dp, axis=1, keepdims=True)) * 0.125
            ds = ds.astype(BF16)
            dqk = jnp.where(low, nn(ds, kk), tn(ds, kk))
            dv = tn(p.astype(BF16), da)
            dot = dqk * QK[l].astype(F32) + dv * vv.astype(F32)
            dot = jnp.sum(dot, axis=1, keepdims=True)
            coef = scale[:, :1] * scale[:, :1] * dot * (1.0 / width)
            sd0 = (dqk * scale).astype(BF16)
            sd1 = (pltpu.roll(dv, 64, 1) * scale).astype(BF16)
            SD[l, 0] = sd0
            SD[l, 1] = sd1

            @pl.when(l > 0)
            def _():
                step_x = nt(jnp.concatenate([sd0, sd1], axis=1), both(l))
                DY[l - 1] = (
                    DY[l].astype(F32) + step_x - X[l].astype(F32) * coef
                ).astype(BF16)

        return carry

    lax.fori_loop(0, layers + 5, backward_step, 0)

    for o in range(1, layers):
        t = section_peer(o)
        send(FS.at[t], OB.at[k, at(SUB * c, SUB)], f_s, f_r, (t, d))
    OB[k, at(SUB * c, SUB)] = FS[s]
    wait(FS.at[pl.ds(0, layers - 1)], f_r)
    out[...] = OB[...]

    wait(W.at[0, 0, pl.ds(0, SUB * (layers - 1))], s1_s)
    wait(mine, y_s)
    if nz > 1:
        for o in range(1, nz):
            wait(W.at[0, :, pl.ds(0, zrows)], z_s)
            wait(H2.at[:, pl.ds(0, zrows)], rz_s)
    if nx > 1:
        for o in range(1, nx):
            wait(W.at[0, :, pl.ds(0, xrows)], x_s)
            wait(H2, rx_s)
    wait(W.at[0], c_s)
    wait(H, rc_s)
    wait(YR, ry_s)
    wait(FS.at[pl.ds(0, layers - 1)], f_s)


def body(nc, nx, nz, inputs, cotangent, doc_lengths, norm_gain, w_qkv, w_out):
    rows, width = inputs.shape[1:]
    layers, dps = 2 * nc, nx * nz * 2
    local = SUB * dps
    grain = SUB * nc
    d = lax.axis_index("dp")
    gain = lax.dynamic_slice(norm_gain[0], (d * grain,), (grain,)).astype(F32)[:, None]
    wq = (w_qkv[0].astype(F32) * gain).astype(BF16)
    wg = jnp.concatenate([wq, w_out[0].T], axis=1)
    wg = jnp.stack([wg[:, :128], wg[:, 128:]])
    vmem = pl.BlockSpec(memory_space=pltpu.VMEM)
    anywhere = pl.BlockSpec(memory_space=pl.ANY)
    dma = pltpu.SemaphoreType.DMA
    xrows, zrows = 2 * SUB * nz, 2 * SUB
    sums = pl.pallas_call(
        functools.partial(kernel, nc, nx, nz, rows),
        out_shape=jax.ShapeDtypeStruct((2, grain, 128), F32),
        in_specs=[anywhere, anywhere, pl.BlockSpec(memory_space=pltpu.SMEM), vmem],
        out_specs=vmem,
        scratch_shapes=[
            pltpu.VMEM((2, layers, local, 128), BF16),
            pltpu.VMEM((rows, width), BF16),
            pltpu.VMEM((rows, width), BF16),
            pltpu.VMEM((layers, rows, local), BF16),
            pltpu.VMEM((layers, rows, local), BF16),
            pltpu.VMEM((layers, rows, 128), BF16),
            pltpu.VMEM((layers, rows, 128), BF16),
            pltpu.VMEM((layers, rows, 128), BF16),
            pltpu.VMEM((layers, rows, rows), F32),
            pltpu.VMEM((layers, rows, 128), BF16),
            pltpu.VMEM((layers, rows, 128), F32),
            pltpu.VMEM((layers, 2, rows, 128), BF16),
            pltpu.VMEM((2, rows, 256), BF16),
            pltpu.VMEM((2, max(nc - 1, 1), rows, 256), BF16),
            pltpu.VMEM((2, rows, 128), BF16),
            pltpu.VMEM((2, max(nc - 1, 1), rows, 128), BF16),
            pltpu.VMEM((layers, 2, local, 128), BF16),
            pltpu.VMEM((layers, local, 128), BF16),
            pltpu.VMEM((layers, local, 128), BF16),
            pltpu.VMEM((layers, max(nx - 1, 1), xrows, 128), BF16),
            pltpu.VMEM((layers, xrows, 128), BF16),
            pltpu.VMEM((layers, max(nz - 1, 1), zrows, 128), BF16),
            pltpu.VMEM((layers, zrows, 128), BF16),
            pltpu.VMEM((layers, SUB, 128), BF16),
            pltpu.VMEM((layers, SUB, 128), F32),
            pltpu.VMEM((2, grain, 128), F32),
            dma((3,)),
            dma, dma, dma, dma,
            dma, dma((layers,)), dma, dma((layers,)), dma, dma((layers,)),
            dma((2,)), dma((2,)), dma((2,)), dma((2,)),
            dma, dma((layers,)), dma, dma((layers,)),
            dma, dma((layers,)), dma, dma((layers,)),
            dma, dma,
        ],
        compiler_params=pltpu.CompilerParams(
            collective_id=0, has_side_effects=True, vmem_limit_bytes=50 * 2**20
        ),
        cost_estimate=pl.CostEstimate(
            flops=24 * layers * rows * local * 256,
            bytes_accessed=4 * rows * width,
            transcendentals=layers * rows * rows,
        ),
    )(inputs, cotangent, doc_lengths[:, 0, :], wg)
    full = jnp.concatenate([sums[0], sums[1]], axis=1)
    return ((full[:, :192] * gain)[None], full[:, 192:].T[None])


def solution(mesh, nx=4, nz=8):
    nc = mesh.shape["section"] // 2
    return jax.shard_map(
        functools.partial(body, nc, nx, nz),
        mesh=mesh,
        in_specs=(
            P(None, "dp", None),
            P(None, "dp", None),
            P(None, "dp", None),
            P("section", None),
            P("section", "dp", None),
            P("section", None, "dp"),
        ),
        out_specs=(P("section", "dp", None), P("section", None, "dp")),
        check_vma=False,
    )
```

time: 1310 us -> 162 us (0.12)
  the two profiles are of different devices: /device:TPU:16 before, /device:TPU:1 now
where the time goes in v1:
time: 162 us; the launch traced here: 161 us
  Pallas kernels  155 us (96%)
  local copies, waits for them, and re-layouts  4 us (2%)
    pallas_call x1, Pallas kernels, body(): pl.pallas_call(functools.partial(kernel, nc, nx, nz, rows), out_shape=jax...  155 us
    unnamed x12, local copies, waits for them, and re-layouts  3.92 us

profile of v1, /device:TPU:1, one launch (start us, length us, event | category | flops | bytes accessed | tf_op | source)
XLA Modules:
  0.0 161.3 jit_solution(14163870835753651136)
XLA Ops:
  0.6 0.0 copy-start.4
  0.6 0.0 copy-start.3
  0.7 0.7 bitcast_convert_fusion
  1.4 0.0 copy-done.4
  1.4 0.1 copy.8
  1.5 0.0 copy-done.3
  1.5 0.1 fusion.2
  1.6 0.1 slice_bitcast_fusion.3
  1.7 0.0 copy-start.2
  1.7 0.7 copy-done.2
  2.3 0.0 copy-start
  2.3 1.2 copy-done
  3.6 0.0 copy-start.1
  3.6 1.2 copy-done.1
  4.8 155.0 %shard_map.77 = f32[2,64,128]{2,1,0:T(8,128)S(1)} custom-call(bf16[2,64,4096]{2,1,0:T(8,128)(2,1)S(1)} %copy-done, bf16[2,64,4096]{2,1,0:T(8,128)(2,1)S(1)} %copy-done.1, s32[2,2]{1,0:T(2,128)S(1)} %bitcast.24, bf16[2,64,128]{2,1,0:T(8,128)(2,1)S(1)} %pad_maximum_fusion.1.wg), custom_call_target="tpu_custom_call" | custom-call | flops 3221225472 | bytes 1048576 | tf_op jit(solution)/shard_map/pallas_call | solution.py:367
  159.8 0.7 fusion.1
  160.5 0.1 slice_bitcast_fusion
  160.6 0.7 copy.9
  (2 shorter events, 0.0 us)
Async XLA Ops:
  0.6 0.8 copy-start.4
  0.6 0.8 copy-start.3
  1.7 0.7 copy-start.2
  2.3 1.2 copy-start
  3.6 1.2 copy-start.1

commit v2 on v1

v2 whole, which is shorter than its diff:
```python
import functools

import jax
import jax.numpy as jnp
from jax import lax
from jax.experimental import pallas as pl
from jax.experimental.pallas import tpu as pltpu
from jax.sharding import PartitionSpec as P

MESH = pl.DeviceIdType.MESH
F32, BF16 = jnp.float32, jnp.bfloat16
SUB = 16


def nn(a, b):
    return jnp.dot(a, b, preferred_element_type=F32)


def nt(a, b):
    return lax.dot_general(a, b, (((1,), (1,)), ((), ())), preferred_element_type=F32)


def tn(a, b):
    return lax.dot_general(a, b, (((0,), (0,)), ((), ())), preferred_element_type=F32)


def kernel(
    nc, nx, nz, rows,
    inp, cot, lens, wg, out,
    W, xin, cin, X, DY, QK, KK, VV, PR, ATT, SC, SD, GM, UA,
    es, er, bs, br, gs, gr, G, SR, H, XR, H2, ZR, TALLY, TALLYB, FS, OB,
    in_sem, s1_s, s1_r, z_s, z_r, x_s, x_r, c_s, c_r,
    e_s, e_r, b_s, b_r, g_s, g_r, rc_s, rc_r, rx_s, rx_r, rz_s, rz_r, f_s, f_r,
):
    layers, pairs = 2 * nc, nc
    dps = nx * nz * 2
    local = SUB * dps
    width = local * nc
    zrows, xrows = 2 * SUB, 2 * SUB * nz
    s, d = lax.axis_index("section"), lax.axis_index("dp")
    c, k = lax.div(s, 2), lax.rem(s, 2)
    x, z, y = lax.div(d, 2 * nz), lax.rem(lax.div(d, 2), nz), lax.rem(d, 2)

    def at(start, size):
        return pl.ds(pl.multiple_of(start, SUB), size)

    def two(m):
        return pl.ds(2 * m, 2)

    def dp_of(px, pz, py):
        return (px * nz + pz) * 2 + py

    def far_first(n):
        return sorted(range(1, n), key=lambda o: -min(o, n - o))

    def column_peer(o):
        n = lax.rem(y * layers + s + o, 2 * layers)
        return lax.rem(n, layers), lax.div(n, layers)

    def chip_peer(o):
        return (2 * lax.rem(c + o, nc) + k, d)

    def x_peer(o):
        return lax.rem(x + o, nx)

    def z_peer(o):
        return lax.rem(z + o, nz)

    sibling = (2 * c + 1 - k, d)

    def send(src, dst, send_sem, recv_sem, device):
        pltpu.make_async_remote_copy(
            src_ref=src, dst_ref=dst, send_sem=send_sem, recv_sem=recv_sem,
            device_id=device, device_id_type=MESH,
        ).start()

    def wait(ref, sem):
        pltpu.make_async_copy(ref, ref, sem).wait()

    load_x = pltpu.make_async_copy(inp.at[k], xin, in_sem.at[0])
    load_c = pltpu.make_async_copy(cot.at[k], cin, in_sem.at[1])
    own = pltpu.make_async_copy(
        wg.at[k, at(SUB * c, SUB)], W.at[k, s, at(SUB * d, SUB)], in_sem.at[2]
    )
    load_x.start()
    load_c.start()
    own.start()

    barrier = pltpu.get_barrier_semaphore()
    peers = []
    for o in range(1, 2 * layers):
        t, ty = column_peer(o)
        peers += [(t, dp_of(x, z, ty))]
    peers += [(s, dp_of(x_peer(o), z, y)) for o in range(1, nx)]
    peers += [(s, dp_of(x, z_peer(o), y)) for o in range(1, nz)]
    for peer in peers:
        pl.semaphore_signal(barrier, inc=1, device_id=peer, device_id_type=MESH)
    grain = min(8, dps)
    big, small = grain * SUB * nc, grain * SUB
    at_row = lax.broadcasted_iota(jnp.int32, (big, small), 0)
    at_lane = lax.broadcasted_iota(jnp.int32, (big, small), 1)
    inside = at_lane & (SUB - 1)
    wanted = (at_lane - inside) * nc + inside + SUB * c
    pick = jnp.where(at_row == wanted, 1.0, 0.0).astype(BF16)

    def picked(source, m):
        return nn(source[:, m * big : (m + 1) * big], pick).astype(BF16)

    load_x.wait()
    for m in range(dps // grain):
        X[0, :, m * small : (m + 1) * small] = picked(xin, m)

    pl.semaphore_wait(barrier, len(peers))

    for o in range(1, 2 * layers):
        t, ty = column_peer(o)
        tc, tk = lax.div(t, 2), lax.rem(t, 2)
        send(
            wg.at[tk, at(SUB * tc, SUB)], W.at[tk, s, at(SUB * d, SUB)],
            s1_s, s1_r, (t, dp_of(x, z, ty)),
        )

    own.wait()
    columns = TALLYB.at[pl.ds(0, 2 * layers - 1)]
    wait(columns, s1_r)

    def z_gather(m):
        block = W.at[k, two(m), at(zrows * (x * nz + z), zrows)]
        for o in far_first(nz):
            send(block, block, z_s, z_r.at[m], (s, dp_of(x, z_peer(o), y)))

    def z_arrived(m):
        if nz > 1:
            wait(W.at[0, pl.ds(0, 2), pl.ds(0, zrows * (nz - 1))], z_r.at[m])

    def x_gather(m):
        block = W.at[k, two(m), at(xrows * x, xrows)]
        for o in far_first(nx):
            send(block, block, x_s, x_r.at[m], (s, dp_of(x_peer(o), z, y)))

    def x_arrived(m):
        if nx > 1:
            wait(W.at[0, pl.ds(0, 2), pl.ds(0, xrows * (nx - 1))], x_r.at[m])

    def core_gather(m):
        block = W.at[k, two(m)]
        send(block, block, c_s, c_r.at[m], sibling)

    def gamma(m):
        @pl.when(m > 0)
        def _():
            wait(W.at[0, pl.ds(0, 2)], c_r.at[m])

        a, b = 2 * m, 2 * m + 1
        right = jnp.concatenate([W[0, b], W[1, b], W[1, a]], axis=1)
        part = tn(W[1, a], right)[64:]
        gs[m] = part.astype(BF16)
        for o in far_first(nc):
            send(gs.at[m], gr.at[m, o - 1], g_s.at[m], g_r.at[m], chip_peer(o))

    def gamma_sum(m):
        total = gs[m].astype(F32)
        if nc > 1:
            wait(gr.at[m], g_r.at[m])
            for o in range(nc - 1):
                total = total + gr[m, o].astype(F32)
            wait(gr.at[m], g_s.at[m])
        GM[m, :64] = jnp.zeros((64, 384), BF16)
        GM[m, 64:] = total.astype(BF16)

    row = lax.broadcasted_iota(jnp.int32, (rows, rows), 0)
    col = lax.broadcasted_iota(jnp.int32, (rows, rows), 1)
    first = lens[k, 0]
    allowed = ((row < first) == (col < first)) & (row >= col)
    lane = lax.broadcasted_iota(jnp.int32, (rows, 128), 1)
    low = lane < 64

    def both(l):
        return jnp.concatenate([W[0, l], W[1, l]], axis=1)

    def attend(l, t0, t1, square):
        scale = lax.rsqrt(square * (1.0 / width) + 1e-05)
        q = t0 * scale
        kk = pltpu.roll(q, 64, 1).astype(BF16)
        vv = pltpu.roll(jnp.where(low, t1 * scale, 0.0), 64, 1).astype(BF16)
        scores = nt(jnp.where(low, q, 0.0).astype(BF16), kk) * 0.125
        scores = jnp.where(allowed, scores, -1e30)
        top = jnp.max(scores, axis=1, keepdims=True)
        e = jnp.exp(scores - top)
        p = e / jnp.sum(e, axis=1, keepdims=True)
        att = nn(p.astype(BF16), vv).astype(BF16)
        QK[l] = q.astype(BF16)
        KK[l] = kk
        VV[l] = vv
        PR[l] = p
        ATT[l] = att
        SC[l] = jnp.broadcast_to(scale, (rows, 128))
        return att

    def forward(m):
        slot = lax.rem(m, 2)
        a, b = 2 * m, 2 * m + 1
        xb = X[a]
        part = nn(xb, jnp.concatenate([both(a), both(b)], axis=1))
        wide = xb.astype(F32)
        square = jnp.sum(wide * wide, axis=1, keepdims=True)
        upper = square.astype(BF16).astype(F32)
        es[slot, :, :384] = part[:, :384].astype(BF16)
        tail = jnp.where(lane < 96, upper, square - upper)
        es[slot, :, 384:] = jnp.where(low, part[:, 384:], tail).astype(BF16)
        for o in far_first(nc):
            send(es.at[slot], er.at[slot, o - 1], e_s.at[slot], e_r.at[slot], chip_peer(o))
        between(m)
        gamma_sum(m)
        t = [part[:, 128 * i : 128 * (i + 1)] for i in range(4)]
        if nc > 1:
            wait(er.at[slot], e_r.at[slot])
            for o in range(nc - 1):
                for i in range(4):
                    t[i] = t[i] + er[slot, o, :, 128 * i : 128 * (i + 1)].astype(F32)
                more = er[slot, o, :, 384:].astype(F32)
                square = square + more[:, 64:65] + more[:, 96:97]
            wait(er.at[slot], e_s.at[slot])
        att = attend(a, t[0], t[1], square)
        u = nn(att, GM[m])
        into = jnp.where(low, 0.0, t[1])
        after = into + jnp.where(low, 0.0, u[:, 256:])
        UA[m] = after
        square = square + jnp.sum(att.astype(F32) * (into + after), axis=1, keepdims=True)
        last = attend(b, t[2] + u[:, :128], t[3] + u[:, 128:256], square)
        middle = (X[a].astype(F32) + nt(att, W[1, a])).astype(BF16)
        X[b] = middle

        @pl.when(m < pairs - 1)
        def _():
            X[b + 1] = (middle.astype(F32) + nt(last, W[1, b])).astype(BF16)

    def between(m):
        @pl.when(m == 0)
        def _():
            gamma(0)

        @pl.when(m + 2 < pairs)
        def _():
            z_arrived(m + 2)
            x_gather(m + 2)

        @pl.when(m + 3 < pairs)
        def _():
            z_gather(m + 3)

        @pl.when(m + 1 < pairs)
        def _():
            x_arrived(m + 1)
            core_gather(m + 1)
            gamma(m + 1)

    z_gather(0)
    load_c.wait()
    for m in range(dps // grain):
        DY[layers - 1, :, m * small : (m + 1) * small] = picked(cin, m)
    z_arrived(0)
    x_gather(0)
    if pairs > 1:
        z_gather(1)
        z_arrived(1)
        x_gather(1)
    if pairs > 2:
        z_gather(2)
    x_arrived(0)
    core_gather(0)
    wait(W.at[0, pl.ds(0, 2)], c_r.at[0])

    def forward_step(m, carry):
        forward(m)
        return carry

    lax.fori_loop(0, pairs, forward_step, 0)

    def grads(m):
        for l in (2 * m, 2 * m + 1):
            left = jnp.concatenate([X[l], DY[l]], axis=0)
            att = ATT[l]
            right = jnp.concatenate(
                [
                    jnp.concatenate([SD[l, 0], SD[l, 1]], axis=1),
                    jnp.concatenate([jnp.zeros_like(att), att], axis=1),
                ],
                axis=0,
            )
            g = tn(left, right)
            G[0, l] = g[:, :128].astype(BF16)
            G[1, l] = g[:, 128:].astype(BF16)
        send(G.at[1 - k, two(m)], SR.at[two(m)], rc_s, rc_r.at[m], sibling)

    def x_scatter(m):
        wait(SR.at[two(m)], rc_r.at[m])
        H[two(m)] = (G[k, two(m)].astype(F32) + SR[two(m)].astype(F32)).astype(BF16)
        for o in far_first(nx):
            px = x_peer(o)
            send(
                H.at[two(m), at(xrows * px, xrows)], XR.at[m, o - 1],
                rx_s, rx_r.at[m], (s, dp_of(px, z, y)),
            )

    def z_scatter(m):
        total = H[two(m), at(xrows * x, xrows)].astype(F32)
        if nx > 1:
            wait(XR.at[m], rx_r.at[m])
            for o in range(nx - 1):
                total = total + XR[m, o].astype(F32)
        H2[two(m)] = total.astype(BF16)
        for o in far_first(nz):
            pz = z_peer(o)
            send(
                H2.at[two(m), at(zrows * pz, zrows)], ZR.at[m, o - 1],
                rz_s, rz_r.at[m], (s, dp_of(x, pz, y)),
            )

    def finish(m):
        total = H2[two(m), at(zrows * z, zrows)].astype(F32)
        if nz > 1:
            wait(ZR.at[m], rz_r.at[m])
            for o in range(nz - 1):
                total = total + ZR[m, o].astype(F32)
        FS[two(m)] = total

    def staged(m, behind, stage):
        @pl.when((m + behind >= 0) & (m + behind < pairs))
        def _():
            stage(m + behind)

    def attend_back(l, da):
        da = jnp.where(low, 0.0, da).astype(BF16)
        vv, kk, p, scale = VV[l], KK[l], PR[l], SC[l]
        dp = nt(da, vv)
        ds = p * (dp - jnp.sum(p * dp, axis=1, keepdims=True)) * 0.125
        ds = ds.astype(BF16)
        dqk = jnp.where(low, nn(ds, kk), tn(ds, kk))
        dv = tn(p.astype(BF16), da)
        dot = dqk * QK[l].astype(F32) + dv * vv.astype(F32)
        dot = jnp.sum(dot, axis=1, keepdims=True)
        coef = scale[:, :1] * scale[:, :1] * dot * (1.0 / width)
        sd0 = (dqk * scale).astype(BF16)
        sd1 = (pltpu.roll(dv, 64, 1) * scale).astype(BF16)
        SD[l, 0] = sd0
        SD[l, 1] = sd1
        return jnp.concatenate([sd0, sd1], axis=1), coef

    def down(l, sd, coef):
        change = nt(sd, both(l)) - X[l].astype(F32) * coef
        DY[l - 1] = (DY[l].astype(F32) + change).astype(BF16)

    def backward_step(step, carry):
        m = pairs - 1 - step
        slot = lax.rem(step, 2)
        a, b = 2 * m, 2 * m + 1

        @pl.when(m >= 0)
        def _():
            part = nn(DY[b], jnp.concatenate([W[1, b], W[1, a]], axis=1))
            part = jnp.where(low, pltpu.roll(part[:, 128:], 64, 1), part[:, :128])
            bs[slot] = part.astype(BF16)
            for o in far_first(nc):
                send(bs.at[slot], br.at[slot, o - 1], b_s.at[slot], b_r.at[slot], chip_peer(o))

        staged(m, 1, grads)
        staged(m, 2, z_scatter)
        staged(m, 1, x_scatter)
        staged(m, 3, finish)

        @pl.when(m >= 0)
        def _():
            total = bs[slot].astype(F32)
            if nc > 1:
                wait(br.at[slot], b_r.at[slot])
                for o in range(nc - 1):
                    total = total + br[slot, o].astype(F32)
                wait(br.at[slot], b_s.at[slot])
            sd, coef = attend_back(b, total)
            other = nt(sd, GM[m, :, :256]) - UA[m] * coef
            down(b, sd, coef)
            sd, coef = attend_back(a, pltpu.roll(total, 64, 1) + other)

            @pl.when(m > 0)
            def _():
                down(a, sd, coef)

        return carry

    lax.fori_loop(0, pairs + 3, backward_step, 0)

    for o in range(1, 2 * layers):
        t, ty = column_peer(o)
        send(
            FS.at[t, at(SUB * ty, SUB)], OB.at[y, k, at(SUB * c, SUB)],
            f_s, f_r, (t, dp_of(x, z, ty)),
        )
    OB[y, k, at(SUB * c, SUB)] = FS[s, at(SUB * y, SUB)]
    wait_f = TALLY.at[pl.ds(0, 2 * layers - 1)]
    wait(wait_f, f_r)
    out[...] = OB[0] + OB[1]

    wait(columns, s1_s)
    if nz > 1:
        for o in range(1, nz):
            wait(W.at[0, :, pl.ds(0, zrows)], z_s)
            wait(H2.at[:, pl.ds(0, zrows)], rz_s)
    if nx > 1:
        for o in range(1, nx):
            wait(W.at[0, :, pl.ds(0, xrows)], x_s)
            wait(H2, rx_s)
    wait(W.at[0], c_s)
    wait(H, rc_s)
    wait(wait_f, f_s)


def body(nc, nx, nz, inputs, cotangent, doc_lengths, norm_gain, w_qkv, w_out):
    rows, width = inputs.shape[1:]
    layers, pairs, dps = 2 * nc, nc, nx * nz * 2
    local = SUB * dps
    grain = SUB * nc
    d = lax.axis_index("dp")
    gain = lax.dynamic_slice(norm_gain[0], (d * grain,), (grain,)).astype(F32)[:, None]
    wq = (w_qkv[0].astype(F32) * gain).astype(BF16)
    wg = jnp.concatenate([wq, w_out[0].T], axis=1)
    wg = jnp.stack([wg[:, :128], wg[:, 128:]])
    vmem = pl.BlockSpec(memory_space=pltpu.VMEM)
    anywhere = pl.BlockSpec(memory_space=pl.ANY)
    dma = pltpu.SemaphoreType.DMA
    xrows, zrows = 2 * SUB * nz, 2 * SUB
    sums = pl.pallas_call(
        functools.partial(kernel, nc, nx, nz, rows),
        out_shape=jax.ShapeDtypeStruct((2, grain, 128), F32),
        in_specs=[anywhere, anywhere, pl.BlockSpec(memory_space=pltpu.SMEM), vmem],
        out_specs=vmem,
        scratch_shapes=[
            pltpu.VMEM((2, layers, local, 128), BF16),
            pltpu.VMEM((rows, width), BF16),
            pltpu.VMEM((rows, width), BF16),
            pltpu.VMEM((layers, rows, local), BF16),
            pltpu.VMEM((layers, rows, local), BF16),
            pltpu.VMEM((layers, rows, 128), BF16),
            pltpu.VMEM((layers, rows, 128), BF16),
            pltpu.VMEM((layers, rows, 128), BF16),
            pltpu.VMEM((layers, rows, rows), F32),
            pltpu.VMEM((layers, rows, 128), BF16),
            pltpu.VMEM((layers, rows, 128), F32),
            pltpu.VMEM((layers, 2, rows, 128), BF16),
            pltpu.VMEM((pairs, 128, 384), BF16),
            pltpu.VMEM((pairs, rows, 128), F32),
            pltpu.VMEM((2, rows, 512), BF16),
            pltpu.VMEM((2, max(nc - 1, 1), rows, 512), BF16),
            pltpu.VMEM((2, rows, 128), BF16),
            pltpu.VMEM((2, max(nc - 1, 1), rows, 128), BF16),
            pltpu.VMEM((pairs, 64, 384), BF16),
            pltpu.VMEM((pairs, max(nc - 1, 1), 64, 384), BF16),
            pltpu.VMEM((2, layers, local, 128), BF16),
            pltpu.VMEM((layers, local, 128), BF16),
            pltpu.VMEM((layers, local, 128), BF16),
            pltpu.VMEM((pairs, max(nx - 1, 1), 2, xrows, 128), BF16),
            pltpu.VMEM((layers, xrows, 128), BF16),
            pltpu.VMEM((pairs, max(nz - 1, 1), 2, zrows, 128), BF16),
            pltpu.VMEM((2 * layers, SUB, 128), F32),
            pltpu.VMEM((2 * layers, SUB, 128), BF16),
            pltpu.VMEM((layers, zrows, 128), F32),
            pltpu.VMEM((2, 2, grain, 128), F32),
            dma((3,)),
            dma, dma,
            dma, dma((pairs,)), dma, dma((pairs,)), dma, dma((pairs,)),
            dma((2,)), dma((2,)), dma((2,)), dma((2,)), dma((pairs,)), dma((pairs,)),
            dma, dma((pairs,)), dma, dma((pairs,)), dma, dma((pairs,)),
            dma, dma,
        ],
        compiler_params=pltpu.CompilerParams(
            collective_id=0, has_side_effects=True, vmem_limit_bytes=60 * 2**20
        ),
        cost_estimate=pl.CostEstimate(
            flops=24 * layers * rows * local * 256,
            bytes_accessed=4 * rows * width,
            transcendentals=layers * rows * rows,
        ),
    )(inputs, cotangent, doc_lengths[:, 0, :], wg)
    full = jnp.concatenate([sums[0], sums[1]], axis=1)
    return ((full[:, :192] * gain)[None], full[:, 192:].T[None])


def solution(mesh, nx=4, nz=8):
    nc = mesh.shape["section"] // 2
    return jax.shard_map(
        functools.partial(body, nc, nx, nz),
        mesh=mesh,
        in_specs=(
            P(None, "dp", None),
            P(None, "dp", None),
            P(None, "dp", None),
            P("section", None),
            P("section", "dp", None),
            P("section", None, "dp"),
        ),
        out_specs=(P("section", "dp", None), P("section", None, "dp")),
        check_vma=False,
    )
```

time: 162 us -> 141 us (0.87)
  Pallas kernels: 155 us -> 136 us
  local copies, waits for them, and re-layouts: 4 us -> 1.66 us
    pallas_call x1, Pallas kernels: 155 us -> 136 us  [body(): pl.pallas_call(functools.partial(kernel, nc, nx, nz, rows), out_shape=jax...]
    unnamed x12 -> x6, local copies, waits for them, and re-layouts: 3.92 us -> 0.8 us
where the time goes in v2:
time: 141 us
  Pallas kernels  136 us (96%)
  other arithmetic  2.22 us (2%)
  local copies, waits for them, and re-layouts  1.66 us (1%)
    pallas_call x1, Pallas kernels, body(): pl.pallas_call(functools.partial(kernel, nc, nx, nz, rows), out_shape=jax...  136 us

profile of v2, /device:TPU:1, one launch (start us, length us, event | category | flops | bytes accessed | tf_op | source)
XLA Modules:
  0.0 140.8 jit_solution(16815334605248942724)
XLA Ops:
  0.6 0.0 copy-start.1
  0.6 0.0 copy-start
  0.7 0.7 bitcast_convert_fusion
  1.4 0.0 copy-done.1
  1.4 0.1 copy.8
  1.5 0.0 copy-done
  1.5 0.1 fusion.2
  1.6 0.1 slice_bitcast_fusion.3
  1.7 0.6 pad_maximum_fusion.1.wg
  2.3 136.2 %shard_map.77 = f32[2,64,128]{2,1,0:T(8,128)} custom-call(bf16[2,64,4096]{2,1,0:T(8,128)(2,1)} %inp.1, bf16[2,64,4096]{2,1,0:T(8,128)(2,1)} %cot.1, s32[2,2]{1,0:T(2,128)} %bitcast.25, bf16[2,64,128]{2,1,0:T(8,128)(2,1)} %pad_maximum_fusion.1.wg), custom_call_target="tpu_custom_call" | custom-call | flops 3221225472 | bytes 1048576 | tf_op jit(solution)/shard_map/pallas_call | solution.py:432
  138.5 0.8 slice_bitcast_fusion.2
  139.3 0.7 fusion.1
  140.0 0.1 slice_bitcast_fusion
  140.1 0.7 copy.9
Async XLA Ops:
  0.6 0.8 copy-start.1
  0.6 0.8 copy-start

commit v3 on v2

--- a/solution.py
+++ b/solution.py
@@ -30,7 +30,7 @@
     W, xin, cin, X, DY, QK, KK, VV, PR, ATT, SC, SD, GM, UA,
     es, er, bs, br, gs, gr, G, SR, H, XR, H2, ZR, TALLY, TALLYB, FS, OB,
     in_sem, s1_s, s1_r, z_s, z_r, x_s, x_r, c_s, c_r,
-    e_s, e_r, b_s, b_r, g_s, g_r, rc_s, rc_r, rx_s, rx_r, rz_s, rz_r, f_s, f_r,
+    e_s, e_r, b_s, b_r, g_s, g_r, h_s, h_r, rc_s, rc_r, rx_s, rx_r, rz_s, rz_r, f_s, f_r,
 ):
     layers, pairs = 2 * nc, nc
     dps = nx * nz * 2
@@ -146,6 +146,8 @@
         block = W.at[k, two(m)]
         send(block, block, c_s, c_r.at[m], sibling)
 
+    half = at(32 * k, 32)
+
     def gamma(m):
         @pl.when(m > 0)
         def _():
@@ -156,17 +158,23 @@
         part = tn(W[1, a], right)[64:]
         gs[m] = part.astype(BF16)
         for o in far_first(nc):
-            send(gs.at[m], gr.at[m, o - 1], g_s.at[m], g_r.at[m], chip_peer(o))
+            send(gs.at[m, half], gr.at[m, o - 1], g_s.at[m], g_r.at[m], chip_peer(o))
 
     def gamma_sum(m):
-        total = gs[m].astype(F32)
+        total = gs[m, half].astype(F32)
         if nc > 1:
             wait(gr.at[m], g_r.at[m])
             for o in range(nc - 1):
                 total = total + gr[m, o].astype(F32)
             wait(gr.at[m], g_s.at[m])
         GM[m, :64] = jnp.zeros((64, 384), BF16)
-        GM[m, 64:] = total.astype(BF16)
+        mine = GM.at[m, at(64 + 32 * k, 32)]
+        mine[...] = total.astype(BF16)
+        send(mine, mine, h_s.at[m], h_r.at[m], sibling)
+
+    def gamma_arrived(m):
+        wait(GM.at[m, pl.ds(64, 32)], h_r.at[m])
+        wait(GM.at[m, pl.ds(64, 32)], h_s.at[m])
 
     row = lax.broadcasted_iota(jnp.int32, (rows, rows), 0)
     col = lax.broadcasted_iota(jnp.int32, (rows, rows), 1)
@@ -222,6 +230,7 @@
                 square = square + more[:, 64:65] + more[:, 96:97]
             wait(er.at[slot], e_s.at[slot])
         att = attend(a, t[0], t[1], square)
+        gamma_arrived(m)
         u = nn(att, GM[m])
         into = jnp.where(low, 0.0, t[1])
         after = into + jnp.where(low, 0.0, u[:, 256:])
@@ -291,17 +300,19 @@
             g = tn(left, right)
             G[0, l] = g[:, :128].astype(BF16)
             G[1, l] = g[:, 128:].astype(BF16)
-        send(G.at[1 - k, two(m)], SR.at[two(m)], rc_s, rc_r.at[m], sibling)
+            send(G.at[1 - k, l], SR.at[l], rc_s, rc_r.at[m], sibling)
 
     def x_scatter(m):
         wait(SR.at[two(m)], rc_r.at[m])
-        H[two(m)] = (G[k, two(m)].astype(F32) + SR[two(m)].astype(F32)).astype(BF16)
-        for o in far_first(nx):
-            px = x_peer(o)
-            send(
-                H.at[two(m), at(xrows * px, xrows)], XR.at[m, o - 1],
-                rx_s, rx_r.at[m], (s, dp_of(px, z, y)),
-            )
+        for i in range(2):
+            l = 2 * m + i
+            H[l] = (G[k, l].astype(F32) + SR[l].astype(F32)).astype(BF16)
+            for o in far_first(nx):
+                px = x_peer(o)
+                send(
+                    H.at[l, at(xrows * px, xrows)], XR.at[m, o - 1, i],
+                    rx_s, rx_r.at[m], (s, dp_of(px, z, y)),
+                )
 
     def z_scatter(m):
         total = H[two(m), at(xrows * x, xrows)].astype(F32)
@@ -365,9 +376,9 @@
                 send(bs.at[slot], br.at[slot, o - 1], b_s.at[slot], b_r.at[slot], chip_peer(o))
 
         staged(m, 1, grads)
+        staged(m, 3, finish)
+        staged(m, 1, x_scatter)
         staged(m, 2, z_scatter)
-        staged(m, 1, x_scatter)
-        staged(m, 3, finish)
 
         @pl.when(m >= 0)
         def _():
@@ -454,7 +465,7 @@
             pltpu.VMEM((2, rows, 128), BF16),
             pltpu.VMEM((2, max(nc - 1, 1), rows, 128), BF16),
             pltpu.VMEM((pairs, 64, 384), BF16),
-            pltpu.VMEM((pairs, max(nc - 1, 1), 64, 384), BF16),
+            pltpu.VMEM((pairs, max(nc - 1, 1), 32, 384), BF16),
             pltpu.VMEM((2, layers, local, 128), BF16),
             pltpu.VMEM((layers, local, 128), BF16),
             pltpu.VMEM((layers, local, 128), BF16),
@@ -469,6 +480,7 @@
             dma, dma,
             dma, dma((pairs,)), dma, dma((pairs,)), dma, dma((pairs,)),
             dma((2,)), dma((2,)), dma((2,)), dma((2,)), dma((pairs,)), dma((pairs,)),
+            dma((pairs,)), dma((pairs,)),
             dma, dma((pairs,)), dma, dma((pairs,)), dma, dma((pairs,)),
             dma, dma,
         ],

time: 141 us -> 135 us (0.957)
  Pallas kernels: 136 us -> 130 us
    pallas_call x1, Pallas kernels: 136 us -> 130 us  [body(): pl.pallas_call(functools.partial(kernel, nc, nx, nz, rows), out_shape=jax...]
where the time goes in v3:
time: 135 us; the launch traced here: 134 us
  Pallas kernels  130 us (96%)
  other arithmetic  2.22 us (2%)
  local copies, waits for them, and re-layouts  1.66 us (1%)
    pallas_call x1, Pallas kernels, body(): pl.pallas_call(functools.partial(kernel, nc, nx, nz, rows), out_shape=jax...  130 us

profile of v3, /device:TPU:1, one launch (start us, length us, event | category | flops | bytes accessed | tf_op | source)
XLA Modules:
  0.0 134.3 jit_solution(1384271186892104016)
XLA Ops:
  0.6 0.0 copy-start.1
  0.6 0.0 copy-start
  0.7 0.7 bitcast_convert_fusion
  1.4 0.0 copy-done.1
  1.4 0.1 copy.8
  1.5 0.0 copy-done
  1.5 0.1 fusion.2
  1.6 0.1 slice_bitcast_fusion.3
  1.7 0.6 pad_maximum_fusion.1.wg
  2.3 129.8 %shard_map.77 = f32[2,64,128]{2,1,0:T(8,128)} custom-call(bf16[2,64,4096]{2,1,0:T(8,128)(2,1)} %inp.1, bf16[2,64,4096]{2,1,0:T(8,128)(2,1)} %cot.1, s32[2,2]{1,0:T(2,128)} %bitcast.25, bf16[2,64,128]{2,1,0:T(8,128)(2,1)} %pad_maximum_fusion.1.wg), custom_call_target="tpu_custom_call" | custom-call | flops 3221225472 | bytes 1048576 | tf_op jit(solution)/shard_map/pallas_call | solution.py:443
  132.1 0.8 slice_bitcast_fusion.2
  132.9 0.7 fusion.1
  133.6 0.1 slice_bitcast_fusion
  133.6 0.7 copy.9
Async XLA Ops:
  0.6 0.8 copy-start.1
  0.6 0.8 copy-start

commit v4 on v3

--- a/solution.py
+++ b/solution.py
@@ -286,33 +286,45 @@
 
     lax.fori_loop(0, pairs, forward_step, 0)
 
+    def grads_of(l):
+        left = jnp.concatenate([X[l], DY[l]], axis=0)
+        att = ATT[l]
+        right = jnp.concatenate(
+            [
+                jnp.concatenate([SD[l, 0], SD[l, 1]], axis=1),
+                jnp.concatenate([jnp.zeros_like(att), att], axis=1),
+            ],
+            axis=0,
+        )
+        g = tn(left, right)
+        G[0, l] = g[:, :128].astype(BF16)
+        G[1, l] = g[:, 128:].astype(BF16)
+        send(G.at[1 - k, l], SR.at[l], rc_s, rc_r.at[l], sibling)
+
+    def scatter_of(m, i):
+        l = 2 * m + i
+        wait(SR.at[l], rc_r.at[l])
+        H[l] = (G[k, l].astype(F32) + SR[l].astype(F32)).astype(BF16)
+        for o in far_first(nx):
+            px = x_peer(o)
+            send(
+                H.at[l, at(xrows * px, xrows)], XR.at[m, o - 1, i],
+                rx_s, rx_r.at[m], (s, dp_of(px, z, y)),
+            )
+
     def grads(m):
-        for l in (2 * m, 2 * m + 1):
-            left = jnp.concatenate([X[l], DY[l]], axis=0)
-            att = ATT[l]
-            right = jnp.concatenate(
-                [
-                    jnp.concatenate([SD[l, 0], SD[l, 1]], axis=1),
-                    jnp.concatenate([jnp.zeros_like(att), att], axis=1),
-                ],
-                axis=0,
-            )
-            g = tn(left, right)
-            G[0, l] = g[:, :128].astype(BF16)
-            G[1, l] = g[:, 128:].astype(BF16)
-            send(G.at[1 - k, l], SR.at[l], rc_s, rc_r.at[m], sibling)
+        @pl.when(m > 0)
+        def _():
+            grads_of(2 * m + 1)
+
+        grads_of(2 * m)
 
     def x_scatter(m):
-        wait(SR.at[two(m)], rc_r.at[m])
-        for i in range(2):
-            l = 2 * m + i
-            H[l] = (G[k, l].astype(F32) + SR[l].astype(F32)).astype(BF16)
-            for o in far_first(nx):
-                px = x_peer(o)
-                send(
-                    H.at[l, at(xrows * px, xrows)], XR.at[m, o - 1, i],
-                    rx_s, rx_r.at[m], (s, dp_of(px, z, y)),
-                )
+        @pl.when(m > 0)
+        def _():
+            scatter_of(m, 1)
+
+        scatter_of(m, 0)
 
     def z_scatter(m):
         total = H[two(m), at(xrows * x, xrows)].astype(F32)
@@ -335,6 +347,22 @@
             for o in range(nz - 1):
                 total = total + ZR[m, o].astype(F32)
         FS[two(m)] = total
+        for i in range(2):
+            for ty in range(2):
+                to_holder(2 * m + i, ty)
+
+    def to_holder(l, ty):
+        here = (l == s) & (y == ty)
+        sums = FS.at[l, pl.ds(SUB * ty, SUB)]
+        place = OB.at[y, k, at(SUB * c, SUB)]
+
+        @pl.when(here)
+        def _():
+            place[...] = sums[...]
+
+        @pl.when(jnp.logical_not(here))
+        def _():
+            send(sums, place, f_s, f_r, (l, dp_of(x, z, ty)))
 
     def staged(m, behind, stage):
         @pl.when((m + behind >= 0) & (m + behind < pairs))
@@ -391,7 +419,16 @@
             sd, coef = attend_back(b, total)
             other = nt(sd, GM[m, :, :256]) - UA[m] * coef
             down(b, sd, coef)
+
+            @pl.when(m == 0)
+            def _():
+                grads_of(b)
+
             sd, coef = attend_back(a, pltpu.roll(total, 64, 1) + other)
+
+            @pl.when(m == 0)
+            def _():
+                scatter_of(m, 1)
 
             @pl.when(m > 0)
             def _():
@@ -401,13 +438,6 @@
 
     lax.fori_loop(0, pairs + 3, backward_step, 0)
 
-    for o in range(1, 2 * layers):
-        t, ty = column_peer(o)
-        send(
-            FS.at[t, at(SUB * ty, SUB)], OB.at[y, k, at(SUB * c, SUB)],
-            f_s, f_r, (t, dp_of(x, z, ty)),
-        )
-    OB[y, k, at(SUB * c, SUB)] = FS[s, at(SUB * y, SUB)]
     wait_f = TALLY.at[pl.ds(0, 2 * layers - 1)]
     wait(wait_f, f_r)
     out[...] = OB[0] + OB[1]
@@ -481,7 +511,7 @@
             dma, dma((pairs,)), dma, dma((pairs,)), dma, dma((pairs,)),
             dma((2,)), dma((2,)), dma((2,)), dma((2,)), dma((pairs,)), dma((pairs,)),
             dma((pairs,)), dma((pairs,)),
-            dma, dma((pairs,)), dma, dma((pairs,)), dma, dma((pairs,)),
+            dma, dma((layers,)), dma, dma((pairs,)), dma, dma((pairs,)),
             dma, dma,
         ],
         compiler_params=pltpu.CompilerParams(

time: 135 us -> 134 us (level)
  no operation moved by 1% of the time
where the time goes in v4:
time: 134 us
  Pallas kernels  129 us (96%)
  other arithmetic  2.22 us (2%)
  local copies, waits for them, and re-layouts  1.66 us (1%)
    pallas_call x1, Pallas kernels, body(): pl.pallas_call(functools.partial(kernel, nc, nx, nz, rows), out_shape=jax...  129 us

profile of v4, /device:TPU:1, one launch (start us, length us, event | category | flops | bytes accessed | tf_op | source)
XLA Modules:
  0.0 133.7 jit_solution(1713695740354189494)
XLA Ops:
  0.6 0.0 copy-start.1
  0.6 0.0 copy-start
  0.7 0.7 bitcast_convert_fusion
  1.4 0.0 copy-done.1
  1.4 0.1 copy.8
  1.5 0.0 copy-done
  1.5 0.1 fusion.2
  1.6 0.1 slice_bitcast_fusion.3
  1.7 0.6 pad_maximum_fusion.1.wg
  2.3 129.2 %shard_map.77 = f32[2,64,128]{2,1,0:T(8,128)} custom-call(bf16[2,64,4096]{2,1,0:T(8,128)(2,1)} %inp.1, bf16[2,64,4096]{2,1,0:T(8,128)(2,1)} %cot.1, s32[2,2]{1,0:T(2,128)} %bitcast.25, bf16[2,64,128]{2,1,0:T(8,128)(2,1)} %pad_maximum_fusion.1.wg), custom_call_target="tpu_custom_call" | custom-call | flops 3221225472 | bytes 1048576 | tf_op jit(solution)/shard_map/pallas_call | solution.py:473
  131.4 0.8 slice_bitcast_fusion.2
  132.2 0.7 fusion.1
  132.9 0.1 slice_bitcast_fusion
  133.0 0.7 copy.9
Async XLA Ops:
  0.6 0.8 copy-start.1
  0.6 0.8 copy-start

commit v5 on v4

--- a/solution.py
+++ b/solution.py
@@ -149,10 +149,6 @@
     half = at(32 * k, 32)
 
     def gamma(m):
-        @pl.when(m > 0)
-        def _():
-            wait(W.at[0, pl.ds(0, 2)], c_r.at[m])
-
         a, b = 2 * m, 2 * m + 1
         right = jnp.concatenate([W[0, b], W[1, b], W[1, a]], axis=1)
         part = tn(W[1, a], right)[64:]
@@ -208,6 +204,7 @@
     def forward(m):
         slot = lax.rem(m, 2)
         a, b = 2 * m, 2 * m + 1
+        wait(W.at[0, pl.ds(0, 2)], c_r.at[m])
         xb = X[a]
         part = nn(xb, jnp.concatenate([both(a), both(b)], axis=1))
         wide = xb.astype(F32)
@@ -218,8 +215,8 @@
         es[slot, :, 384:] = jnp.where(low, part[:, 384:], tail).astype(BF16)
         for o in far_first(nc):
             send(es.at[slot], er.at[slot, o - 1], e_s.at[slot], e_r.at[slot], chip_peer(o))
+        gamma(m)
         between(m)
-        gamma_sum(m)
         t = [part[:, 128 * i : 128 * (i + 1)] for i in range(4)]
         if nc > 1:
             wait(er.at[slot], e_r.at[slot])
@@ -229,7 +226,14 @@
                 more = er[slot, o, :, 384:].astype(F32)
                 square = square + more[:, 64:65] + more[:, 96:97]
             wait(er.at[slot], e_s.at[slot])
+        gamma_sum(m)
         att = attend(a, t[0], t[1], square)
+
+        @pl.when(m + 1 < pairs)
+        def _():
+            x_arrived(m + 1)
+            core_gather(m + 1)
+
         gamma_arrived(m)
         u = nn(att, GM[m])
         into = jnp.where(low, 0.0, t[1])
@@ -245,10 +249,6 @@
             X[b + 1] = (middle.astype(F32) + nt(last, W[1, b])).astype(BF16)
 
     def between(m):
-        @pl.when(m == 0)
-        def _():
-            gamma(0)
-
         @pl.when(m + 2 < pairs)
         def _():
             z_arrived(m + 2)
@@ -257,12 +257,6 @@
         @pl.when(m + 3 < pairs)
         def _():
             z_gather(m + 3)
-
-        @pl.when(m + 1 < pairs)
-        def _():
-            x_arrived(m + 1)
-            core_gather(m + 1)
-            gamma(m + 1)
 
     z_gather(0)
     load_c.wait()
@@ -278,8 +272,6 @@
         z_gather(2)
     x_arrived(0)
     core_gather(0)
-    wait(W.at[0, pl.ds(0, 2)], c_r.at[0])
-
     def forward_step(m, carry):
         forward(m)
         return carry

time: 134 us -> 142 us (1.060)
  Pallas kernels: 129 us -> 137 us
    pallas_call x1, Pallas kernels: 129 us -> 137 us  [body(): pl.pallas_call(functools.partial(kernel, nc, nx, nz, rows), out_shape=jax...]
where the time goes in v5:
time: 142 us
  Pallas kernels  137 us (96%)
  other arithmetic  2.22 us (2%)
  local copies, waits for them, and re-layouts  1.66 us (1%)
    pallas_call x1, Pallas kernels, body(): pl.pallas_call(functools.partial(kernel, nc, nx, nz, rows), out_shape=jax...  137 us

profile of v5, /device:TPU:1, one launch (start us, length us, event | category | flops | bytes accessed | tf_op | source)
XLA Modules:
  0.0 142.0 jit_solution(16558576184907093116)
XLA Ops:
  0.6 0.0 copy-start.1
  0.6 0.0 copy-start
  0.7 0.7 bitcast_convert_fusion
  1.4 0.0 copy-done.1
  1.4 0.1 copy.8
  1.5 0.0 copy-done
  1.5 0.1 fusion.2
  1.6 0.1 slice_bitcast_fusion.3
  1.7 0.6 pad_maximum_fusion.1.wg
  2.3 137.5 %shard_map.77 = f32[2,64,128]{2,1,0:T(8,128)} custom-call(bf16[2,64,4096]{2,1,0:T(8,128)(2,1)} %inp.1, bf16[2,64,4096]{2,1,0:T(8,128)(2,1)} %cot.1, s32[2,2]{1,0:T(2,128)} %bitcast.25, bf16[2,64,128]{2,1,0:T(8,128)(2,1)} %pad_maximum_fusion.1.wg), custom_call_target="tpu_custom_call" | custom-call | flops 3221225472 | bytes 1048576 | tf_op jit(solution)/shard_map/pallas_call | solution.py:465
  139.8 0.8 slice_bitcast_fusion.2
  140.5 0.7 fusion.1
  141.2 0.1 slice_bitcast_fusion
  141.3 0.7 copy.9
Async XLA Ops:
  0.6 0.8 copy-start.1
  0.6 0.8 copy-start
